TPU v7x, 512 devices: a whole 4x8x8 slice. The times are simulated.
512 devices in a mesh: fsdp: 4 (over x_hi, core), sp: 8 (over z), enc: 16 (over x_lo, y).
Axes of the slice: x: 4 (x_hi: 2, x_lo: 2; x = x_hi * 2 + x_lo), y: 8, z: 8, core: 2. Of those that a mesh axis runs over, the one named last changes fastest.
Arguments:
- image_qkv: bfloat16 [64, 1024, 3, 2048], P(('fsdp', 'enc'), 'sp'), may hold values from -6 to 6
- cotangent: bfloat16 [64, 1024, 2048], P(('fsdp', 'enc'), 'sp'), may hold values from -320 to 320
- text_kv: bfloat16 [8192, 2, 2048], P(('fsdp', 'sp', 'enc')), may hold values from -6 to 6
- routes: int32 [8192, 1], P(('fsdp', 'sp', 'enc')), may hold values from 0 to 15; in each aligned block of 16 rows (0 to 15, 16 to 31, ...) at most 2 rows name the same one
- q_gain: float32 [128], replicated, may hold values from 0.1 to 1.9
- k_gain: float32 [128], replicated, may hold values from 0.1 to 1.9
- text_gain: float32 [128], replicated, may hold values from 0.1 to 1.9
Outputs:
- image_grad: bfloat16 [64, 1024, 3, 2048], P(('fsdp', 'enc'), 'sp')
- text_grad: bfloat16 [8192, 2, 2048], P(('fsdp', 'sp', 'enc'))
- gain_grads: float32 [3, 128], replicated
Inputs may be any that keep to these rules, and one draw needn't show every extreme that they name: `routes`: within the rows of one encoder shard no value appears more than 2 times, and in every draw some shard has a value exactly 2 times.
All inputs are finite; a program needn't handle non-finite values.
Results may differ from a plain program's by a relative error of at most 0.012.
The roundings to bfloat16 on the way count: a program that leaves them out, or rounds other values in their place, can miss the bound.
Values may be sent and summed in bfloat16 or wider, within the bound.
A program may use at most 64 MiB of HBM per device.

v0:
```python
import jax
import jax.numpy as jnp
from jax import lax
from jax.sharding import PartitionSpec as P

EPSILON = 1e-06


def norm_heads(raw_rows, gain_vec):
    wide_rows = raw_rows.astype(jnp.float32)
    factor = lax.rsqrt(jnp.mean(wide_rows * wide_rows, axis=-1, keepdims=True) + EPSILON)
    unit_rows = wide_rows * factor
    return ((unit_rows * gain_vec).astype(jnp.bfloat16), unit_rows, factor)


def norm_back(grad_norm, unit_rows, factor, gain_vec):
    scaled = grad_norm * gain_vec
    inner_mean = jnp.mean(scaled * unit_rows, axis=-1, keepdims=True)
    lead_axes = tuple(range(grad_norm.ndim - 1))
    return (
        factor * (scaled - unit_rows * inner_mean),
        jnp.sum(grad_norm * unit_rows, axis=lead_axes),
    )


def block_weight(query_rows, key_rows, live_mask, score_scale):
    scores = (
        jnp.einsum("qd,kd->qk", query_rows, key_rows, preferred_element_type=jnp.float32)
        * score_scale
    )
    return jnp.exp(scores) * live_mask[None, :]


def attend_block(query_rows, grad_rows, groups, score_scale):
    row_total = jnp.zeros((query_rows.shape[0],), jnp.float32)
    numerator = jnp.zeros(query_rows.shape, jnp.float32)
    saved_packed = []
    for key_rows, value_rows, live_mask in groups:
        weight = block_weight(query_rows, key_rows, live_mask, score_scale)
        row_total = jnp.sum(weight, axis=1)
        packed = weight.astype(jnp.bfloat16)
        numerator = jnp.dot(packed, value_rows, preferred_element_type=jnp.float32)
        saved_packed.append(packed)
    output = numerator / row_total[:, None]
    grad_wide = grad_rows.astype(jnp.float32)
    grad_scaled = (grad_wide / row_total[:, None]).astype(jnp.bfloat16)
    grad_total = -jnp.sum(grad_wide * output, axis=1) / row_total
    grad_query = jnp.zeros(query_rows.shape, jnp.float32)
    key_results = []
    for group_parts, packed in zip(groups, saved_packed):
        key_rows, value_rows, live_mask = group_parts
        weight = block_weight(query_rows, key_rows, live_mask, score_scale)
        back_prod = jnp.einsum(
            "qd,kd->qk", grad_scaled, value_rows, preferred_element_type=jnp.float32
        )
        tangent = ((back_prod + grad_total[:, None]) * weight * score_scale).astype(jnp.bfloat16)
        grad_query = jnp.dot(tangent, key_rows, preferred_element_type=jnp.float32)
        grad_keys = jnp.einsum("qk,qd->kd", tangent, query_rows, preferred_element_type=jnp.float32)
        grad_values = jnp.einsum(
            "qk,qd->kd", packed, grad_scaled, preferred_element_type=jnp.float32
        )
        key_results.append((grad_keys, grad_values))
    return (grad_query, key_results)


def on_device(image_qkv, cotangent, text_kv, routes, q_gain, k_gain, text_gain):
    rows_local = image_qkv.shape[1]
    width = image_qkv.shape[3]
    sp_size = lax.axis_size("sp")
    enc_size = lax.axis_size("enc")
    text_rows = text_kv.shape[0]
    slot_count = 2 * text_rows
    per_dest = slot_count // enc_size
    destination = routes[:, 0]
    dest_table = (destination[:, None] == jnp.arange(enc_size, dtype=jnp.int32)[None, :]).astype(
        jnp.int32
    )
    earlier = jnp.cumsum(dest_table, axis=0) - dest_table
    rank_in_dest = jnp.sum(earlier * dest_table, axis=1)
    slot_index = destination * per_dest + rank_in_dest
    placement = (slot_index[None, :] == jnp.arange(slot_count, dtype=jnp.int32)[:, None]).astype(
        jnp.bfloat16
    )
    send_rows = jnp.dot(
        placement, text_kv.reshape(text_rows, 2 * width), preferred_element_type=jnp.float32
    ).astype(jnp.bfloat16)
    send_rows = send_rows.reshape(enc_size, 1, per_dest, 2, width)
    occupied = jnp.sum(placement.astype(jnp.float32), axis=1).astype(jnp.bfloat16)
    slot_flags = jnp.broadcast_to(
        occupied.reshape(enc_size, 1, per_dest, 1, 1), (enc_size, 1, per_dest, 1, sp_size)
    )
    text_heads, flag_heads = (
        lax.all_to_all(
            lax.all_to_all(send_rows, "sp", split_axis=4, concat_axis=1, tiled=True),
            "enc",
            split_axis=0,
            concat_axis=0,
            tiled=True,
        ),
        lax.all_to_all(
            lax.all_to_all(slot_flags, "sp", split_axis=4, concat_axis=1, tiled=True),
            "enc",
            split_axis=0,
            concat_axis=0,
            tiled=True,
        ),
    )
    grad_input = cotangent.reshape(1, rows_local, 1, width)
    head_qkv, head_grad = (
        lax.all_to_all(image_qkv, "sp", split_axis=3, concat_axis=1, tiled=True),
        lax.all_to_all(grad_input, "sp", split_axis=3, concat_axis=1, tiled=True),
    )
    seq_rows = head_qkv.shape[1]
    head_width = head_qkv.shape[3]
    head_dim = q_gain.shape[0]
    local_heads = head_width // head_dim
    text_keys = text_heads.shape[0] * text_heads.shape[1] * text_heads.shape[2]
    text_block = text_heads.reshape(text_keys, 2, local_heads, head_dim)
    text_live = flag_heads.reshape(text_keys).astype(jnp.float32)
    q_norm, q_unit, q_factor = norm_heads(
        head_qkv[0, :, 0].reshape(seq_rows, local_heads, head_dim), q_gain
    )
    k_norm, k_unit, k_factor = norm_heads(
        head_qkv[0, :, 1].reshape(seq_rows, local_heads, head_dim), k_gain
    )
    v_rows = head_qkv[0, :, 2].reshape(seq_rows, local_heads, head_dim)
    t_norm, t_unit, t_factor = norm_heads(text_block[:, 0], text_gain)
    t_values = text_block[:, 1]
    grad_heads = head_grad[0, :, 0].reshape(seq_rows, local_heads, head_dim)
    block_rows = min(512, seq_rows)
    score_scale = head_dim ** (-0.5)
    image_live = jnp.ones((seq_rows,), jnp.float32)
    dq_list, dk_list, dv_list, dtk_list, dtv_list = ([], [], [], [], [])
    for head_index in range(local_heads):
        groups = [
            (
                jnp.concatenate([k_norm[:, head_index], t_norm[:, head_index]], axis=0),
                jnp.concatenate([v_rows[:, head_index], t_values[:, head_index]], axis=0),
                jnp.concatenate([image_live, text_live]),
            )
        ]
        key_sums = [jnp.zeros(group_parts[0].shape, jnp.float32) for group_parts in groups]
        value_sums = [jnp.zeros(group_parts[0].shape, jnp.float32) for group_parts in groups]
        query_parts = []
        for row_start in range(0, seq_rows, block_rows):
            grad_query, key_results = attend_block(
                q_norm[row_start : row_start + block_rows, head_index],
                grad_heads[row_start : row_start + block_rows, head_index],
                groups,
                score_scale,
            )
            query_parts.append(grad_query)
            key_sums = [
                total_keys + result_pair[0]
                for total_keys, result_pair in zip(key_sums, key_results)
            ]
            value_sums = [
                total_values + result_pair[1]
                for total_values, result_pair in zip(value_sums, key_results)
            ]
        dq_list.append(jnp.concatenate(query_parts, axis=0))
        dk_list.append(key_sums[0][:seq_rows])
        dtk_list.append(key_sums[0][seq_rows:])
        dv_list.append(value_sums[0][:seq_rows])
        dtv_list.append(value_sums[0][seq_rows:])
    dq_rows, q_term = norm_back(jnp.stack(dq_list, axis=1), q_unit, q_factor, q_gain)
    dk_rows, k_term = norm_back(jnp.stack(dk_list, axis=1), k_unit, k_factor, k_gain)
    dt_rows, t_term = norm_back(jnp.stack(dtk_list, axis=1), t_unit, t_factor, text_gain)
    dv_rows = jnp.stack(dv_list, axis=1)
    dtv_rows = jnp.stack(dtv_list, axis=1)
    image_heads_grad = (
        jnp.stack([dq_rows, dk_rows, dv_rows], axis=1)
        .reshape(1, seq_rows, 3, head_width)
        .astype(jnp.bfloat16)
    )
    image_grad = lax.all_to_all(image_heads_grad, "sp", split_axis=1, concat_axis=3, tiled=True)
    text_heads_grad = (
        jnp.stack([dt_rows, dtv_rows], axis=1)
        .reshape(text_heads.shape[0], text_heads.shape[1], text_heads.shape[2], 2, head_width)
        .astype(jnp.bfloat16)
    )
    slot_grads = lax.all_to_all(
        lax.all_to_all(text_heads_grad, "sp", split_axis=1, concat_axis=4, tiled=True),
        "enc",
        split_axis=0,
        concat_axis=0,
        tiled=True,
    )
    slot_grads = slot_grads.reshape(slot_count, 2 * width)
    text_grad = jnp.einsum("sr,sc->rc", placement, slot_grads, preferred_element_type=jnp.float32)
    text_grad = text_grad.astype(jnp.bfloat16).reshape(text_rows, 2, width)
    gain_terms = jnp.stack([q_term, k_term, t_term])
    gain_total = lax.psum(gain_terms, ("fsdp", "sp", "enc"))
    sample_count = lax.axis_size("fsdp") * enc_size
    scale_total = float(sample_count * seq_rows * local_heads * sp_size) ** (-0.5)
    gain_grads = gain_total * scale_total
    return (image_grad, text_grad, gain_grads)


def solution(mesh):
    placed = (
        P(("fsdp", "enc"), "sp", None, None),
        P(("fsdp", "enc"), "sp", None),
        P(("fsdp", "sp", "enc"), None, None),
        P(("fsdp", "sp", "enc"), None),
        P(),
        P(),
        P(),
    )
    return jax.shard_map(
        on_device,
        mesh=mesh,
        in_specs=placed,
        out_specs=(P(("fsdp", "enc"), "sp", None, None), P(("fsdp", "sp", "enc"), None, None), P()),
        check_vma=False,
    )
```

profile of v0, /device:TPU:6, one launch (start us, length us, event | category | flops | bytes accessed | tf_op | source)
XLA Modules:
  0.0 361.0 jit_solution(9437447143996530464)
XLA Ops:
  3.8 10.3 %all-to-all-start.4 = ((bf16[16,1,2,1,8]{0,2,3,1,4:T(2,128)(2,1)}), bf16[16,1,2,1,8]{0,2,3,1,4:T(2,128)(2,1)S(1)}, u32[]{:S(2)}, u32[]{:S(2)}) async-start(bf16[16,1,2,1,8]{0,2,3,1,4:T(2,128)(2,1)} %broadcast_in_dim.5), calls=%async_computation.4 | async-start | bytes 8192 | tf_op jit(solution)/shard_map/all_to_all | solution.py:101
  15.1 6.7 %all-to-all-done.4 = bf16[16,1,2,1,8]{0,2,3,1,4:T(2,128)(2,1)S(1)} async-done(((bf16[16,1,2,1,8]{0,2,3,1,4:T(2,128)(2,1)}), bf16[16,1,2,1,8]{0,2,3,1,4:T(2,128)(2,1)S(1)}, u32[]{:S(2)}, u32[]{:S(2)}) %all-to-all-start.4) | async-done | bytes 544 | tf_op jit(solution)/shard_map/all_to_all | solution.py:101
  22.4 8.6 %all-to-all-start.5 = ((bf16[16,8,2,1,1]{1,2,4,3,0:T(2,128)(2,1)}), bf16[16,8,2,1,1]{1,2,4,3,0:T(2,128)(2,1)S(1)}, u32[]{:S(2)}, u32[]{:S(2)}) async-start(bf16[16,8,2,1,1]{1,2,4,3,0:T(2,128)(2,1)} %copy.138), calls=%async_computation.5 | async-start | bytes 16384 | tf_op jit(solution)/shard_map/all_to_all | solution.py:100
  31.5 3.8 %copy.131 = bf16[16,1,2,2,2048]{0,3,2,1,4:T(2,128)(2,1)} copy(bf16[16,1,2,2,2048]{4,3,2,0,1:T(2,128)(2,1)S(1)} %reshape.374) | data formatting | bytes 524288 | tf_op jit(solution)/shard_map/reshape | solution.py:87
  35.3 4.0 %reshape.386 = bf16[8,2,8192]{2,1,0:T(2,128)(2,1)} reshape(bf16[2048,1,2,2,16]{4,3,2,1,0:T(2,128)(2,1)} %bitcast.238) | data formatting | bytes 524288
  39.3 3.4 all-to-all-start.2
  44.0 11.5 %reduce.5 = bf16[2048,128]{1,0:T(8,128)(2,1)S(1)} reduce(bf16[2048,1,1,128]{3,2,1,0:T(2,128)(2,1)S(1)} %bitcast.248, bf16[]{:T(256)} %broadcast.210), dimensions={1,2}, to_apply=%bitcast.211.reduce_sub_computation | reduce | bytes 1048578
  56.5 7.1 %all-to-all-start.1 = ((bf16[8,2,16384]{2,1,0:T(2,128)(2,1)}), bf16[8,2,16384]{2,1,0:T(2,128)(2,1)S(1)}, u32[]{:S(2)}, u32[]{:S(2)}) async-start(bf16[8,2,16384]{2,1,0:T(2,128)(2,1)} %reshape.388), calls=%async_computation.1 | async-start | bytes 1048576 | tf_op jit(solution)/shard_map/all_to_all | solution.py:111
  66.1 4.1 %copy.152 = bf16[16,1,2,2,8,256]{5,4,3,2,0,1:T(8,128)(2,1)} copy(bf16[16,1,2,2,8,256]{0,3,2,5,4,1:T(2,128)(2,1)} %bitcast.239) | data formatting | bytes 524288 | tf_op jit(solution)/shard_map/all_to_all | solution.py:94
  70.2 8.7 %all-to-all-done.1 = bf16[8,2,16384]{2,1,0:T(2,128)(2,1)S(1)} async-done(((bf16[8,2,16384]{2,1,0:T(2,128)(2,1)}), bf16[8,2,16384]{2,1,0:T(2,128)(2,1)S(1)}, u32[]{:S(2)}, u32[]{:S(2)}) %all-to-all-start.1) | async-done | bytes 524320 | tf_op jit(solution)/shard_map/all_to_all | solution.py:111
  78.8 8.1 %all-to-all-start.3 = ((bf16[16,8,2,2,256]{4,1,3,2,0:T(8,128)(2,1)}), bf16[16,8,2,2,256]{4,1,3,2,0:T(8,128)(2,1)S(1)}, u32[]{:S(2)}, u32[]{:S(2)}) async-start(bf16[16,8,2,2,256]{4,1,3,2,0:T(8,128)(2,1)} %bitcast.14), calls=%async_computation.3 | async-start | bytes 524288 | tf_op jit(solution)/shard_map/all_to_all | solution.py:93
  89.5 5.4 %all-to-all-done.3 = bf16[16,8,2,2,256]{4,1,3,2,0:T(8,128)(2,1)S(1)} async-done(((bf16[16,8,2,2,256]{4,1,3,2,0:T(8,128)(2,1)}), bf16[16,8,2,2,256]{4,1,3,2,0:T(8,128)(2,1)S(1)}, u32[]{:S(2)}, u32[]{:S(2)}) %all-to-all-start.3) | async-done | bytes 262176 | tf_op jit(solution)/shard_map/all_to_all | solution.py:93
  95.0 4.6 %all-to-all-start = ((bf16[1,128,3,2048]{1,2,0,3:T(4,128)(2,1)}), bf16[1,128,3,2048]{1,2,0,3:T(4,128)(2,1)}, u32[]{:S(2)}, u32[]{:S(2)}) async-start(bf16[1,128,3,2048]{1,2,0,3:T(4,128)(2,1)} %copy.125), calls=%async_computation | async-start | bytes 4194304 | tf_op jit(solution)/shard_map/all_to_all | solution.py:110
  103.6 39.8 %all-to-all-done = bf16[1,128,3,2048]{1,2,0,3:T(4,128)(2,1)} async-done(((bf16[1,128,3,2048]{1,2,0,3:T(4,128)(2,1)}), bf16[1,128,3,2048]{1,2,0,3:T(4,128)(2,1)}, u32[]{:S(2)}, u32[]{:S(2)}) %all-to-all-start) | async-done | bytes 1572896 | tf_op jit(solution)/shard_map/all_to_all | solution.py:110
  143.4 4.0 %copy.164 = bf16[1,128,3,8,256]{1,3,4,2,0:T(8,128)(2,1)} copy(bf16[1,128,3,8,256]{1,2,4,3,0:T(4,128)(2,1)} %bitcast) | data formatting | bytes 3145728 | tf_op jit(solution)/shard_map/all_to_all | solution.py:110
  147.4 2.5 all_to_all.88
  152.7 2.5 copy.130
  184.8 4.3 %all-to-all-start.7 = ((bf16[16,8,2,2,256]{4,2,0,3,1:T(2,128)(2,1)}), bf16[16,8,2,2,256]{4,2,0,3,1:T(2,128)(2,1)S(1)}, u32[]{:S(2)}, u32[]{:S(2)}) async-start(bf16[16,8,2,2,256]{4,2,0,3,1:T(2,128)(2,1)} %copy.147), calls=%async_computation.7 | async-start | bytes 524288 | tf_op jit(solution)/shard_map/all_to_all | solution.py:183
  196.4 2.5 copy.142
  202.3 5.5 %all-to-all-start.8 = ((bf16[16,1,2,2,2048]{4,3,2,1,0:T(2,128)(2,1)}), bf16[16,1,2,2,2048]{4,3,2,1,0:T(2,128)(2,1)S(1)}, u32[]{:S(2)}, u32[]{:S(2)}) async-start(bf16[16,1,2,2,2048]{4,3,2,1,0:T(2,128)(2,1)} %reshape.385), calls=%async_computation.8 | async-start | bytes 524288 | tf_op jit(solution)/shard_map/all_to_all | solution.py:182
  210.8 2.6 copy.143
  215.8 6.6 %all-to-all-start.6 = ((bf16[1,1024,3,256]{3,2,0,1:T(4,128)(2,1)}), bf16[1,1024,3,256]{3,2,0,1:T(4,128)(2,1)}, u32[]{:S(2)}, u32[]{:S(2)}) async-start(bf16[1,1024,3,256]{3,2,0,1:T(4,128)(2,1)} %copy.143), calls=%async_computation.6 | async-start | bytes 4194304 | tf_op jit(solution)/shard_map/all_to_all | solution.py:176
  222.5 132.0 %psum.7 = f32[3,128]{1,0:T(4,128)S(1)} all-reduce(f32[3,128]{1,0:T(4,128)S(1)} %pad_maximum_fusion.15), channel_id=1, replica_groups=mesh['fsdp'=4,'sp'=8,'enc'=16] {'fsdp','sp','enc'}, use_global_device_ids=true, to_apply=%region_22.23 | all-reduce | flops 384 | bytes 3072 | tf_op jit(solution)/shard_map/psum | solution.py:193
  356.2 2.7 copy.144
  (176 shorter events, 68.1 us)
Async XLA Ops:
  2.9 28.1 %copy-start.26 = (s32[16]{0:T(128)}, s32[16]{0:T(128)S(1)}, u32[]{:S(2)}) copy-start(s32[16]{0:T(128)S(1)} %multiply_add_fusion) | copy-start | bytes 196
  3.8 17.9 %all-to-all-start.4 = ((bf16[16,1,2,1,8]{0,2,3,1,4:T(2,128)(2,1)}), bf16[16,1,2,1,8]{0,2,3,1,4:T(2,128)(2,1)S(1)}, u32[]{:S(2)}, u32[]{:S(2)}) async-start(bf16[16,1,2,1,8]{0,2,3,1,4:T(2,128)(2,1)} %broadcast_in_dim.5), calls=%async_computation.4 | async-start | bytes 8192 | tf_op jit(solution)/shard_map/all_to_all | solution.py:101
  22.4 16.9 %all-to-all-start.5 = ((bf16[16,8,2,1,1]{1,2,4,3,0:T(2,128)(2,1)}), bf16[16,8,2,1,1]{1,2,4,3,0:T(2,128)(2,1)S(1)}, u32[]{:S(2)}, u32[]{:S(2)}) async-start(bf16[16,8,2,1,1]{1,2,4,3,0:T(2,128)(2,1)} %copy.138), calls=%async_computation.5 | async-start | bytes 16384 | tf_op jit(solution)/shard_map/all_to_all | solution.py:100
  31.5 11.3 %copy-start.12 = (bf16[1,128,2048]{2,1,0:T(8,128)(2,1)S(1)}, bf16[1,128,2048]{2,1,0:T(8,128)(2,1)}, u32[]{:S(2)}) copy-start(bf16[1,128,2048]{2,1,0:T(8,128)(2,1)} %param.8) | copy-start | bytes 1572868
  39.3 17.2 %all-to-all-start.2 = ((bf16[8,2,8192]{2,1,0:T(2,128)(2,1)}), bf16[8,2,8192]{2,1,0:T(2,128)(2,1)S(1)}, u32[]{:S(2)}, u32[]{:S(2)}) async-start(bf16[8,2,8192]{2,1,0:T(2,128)(2,1)} %reshape.386), calls=%async_computation.2 | async-start | bytes 524288 | tf_op jit(solution)/shard_map/all_to_all | solution.py:94
  56.5 22.3 %all-to-all-start.1 = ((bf16[8,2,16384]{2,1,0:T(2,128)(2,1)}), bf16[8,2,16384]{2,1,0:T(2,128)(2,1)S(1)}, u32[]{:S(2)}, u32[]{:S(2)}) async-start(bf16[8,2,16384]{2,1,0:T(2,128)(2,1)} %reshape.388), calls=%async_computation.1 | async-start | bytes 1048576 | tf_op jit(solution)/shard_map/all_to_all | solution.py:111
  63.6 23.4 %copy-start.9 = (bf16[1,128,3,2048]{3,1,2,0:T(8,128)(2,1)S(1)}, bf16[1,128,3,2048]{3,1,2,0:T(8,128)(2,1)}, u32[]{:S(2)}) copy-start(bf16[1,128,3,2048]{3,1,2,0:T(8,128)(2,1)} %param.7) | copy-start | bytes 4718596
  78.8 16.1 %all-to-all-start.3 = ((bf16[16,8,2,2,256]{4,1,3,2,0:T(8,128)(2,1)}), bf16[16,8,2,2,256]{4,1,3,2,0:T(8,128)(2,1)S(1)}, u32[]{:S(2)}, u32[]{:S(2)}) async-start(bf16[16,8,2,2,256]{4,1,3,2,0:T(8,128)(2,1)} %bitcast.14), calls=%async_computation.3 | async-start | bytes 524288 | tf_op jit(solution)/shard_map/all_to_all | solution.py:93
  89.5 10.0 %copy-start.20 = (f32[128]{0:T(128)S(1)}, f32[128]{0:T(128)}, u32[]{:S(2)}) copy-start(f32[128]{0:T(128)} %param.12) | copy-start | bytes 1540
  89.5 10.0 %copy-start.21 = (f32[128]{0:T(128)S(1)}, f32[128]{0:T(128)}, u32[]{:S(2)}) copy-start(f32[128]{0:T(128)} %param.11) | copy-start | bytes 1540
  95.0 48.5 %all-to-all-start = ((bf16[1,128,3,2048]{1,2,0,3:T(4,128)(2,1)}), bf16[1,128,3,2048]{1,2,0,3:T(4,128)(2,1)}, u32[]{:S(2)}, u32[]{:S(2)}) async-start(bf16[1,128,3,2048]{1,2,0,3:T(4,128)(2,1)} %copy.125), calls=%async_computation | async-start | bytes 4194304 | tf_op jit(solution)/shard_map/all_to_all | solution.py:110
  103.5 44.0 %copy-start.17 = (f32[256,2]{0,1:T(2,128)}, f32[256,2]{0,1:T(2,128)S(1)}, u32[]{:S(2)}) copy-start(f32[256,2]{0,1:T(2,128)S(1)} %add_rsqrt_fusion.2) | copy-start | bytes 6148
  184.8 14.8 %all-to-all-start.7 = ((bf16[16,8,2,2,256]{4,2,0,3,1:T(2,128)(2,1)}), bf16[16,8,2,2,256]{4,2,0,3,1:T(2,128)(2,1)S(1)}, u32[]{:S(2)}, u32[]{:S(2)}) async-start(bf16[16,8,2,2,256]{4,2,0,3,1:T(2,128)(2,1)} %copy.147), calls=%async_computation.7 | async-start | bytes 524288 | tf_op jit(solution)/shard_map/all_to_all | solution.py:183
  189.1 3.7 %copy-start.13 = (f32[512,128]{1,0:T(8,128)S(1)}, f32[512,128]{1,0:T(8,128)}, u32[]{:S(2)}) copy-start(f32[512,128]{1,0:T(8,128)} %fusion.77) | copy-start | bytes 786436
  189.1 3.7 %copy-start.14 = (f32[512,128]{1,0:T(8,128)S(1)}, f32[512,128]{1,0:T(8,128)}, u32[]{:S(2)}) copy-start(f32[512,128]{1,0:T(8,128)} %fusion.75) | copy-start | bytes 786436
  189.1 3.6 %copy-start.15 = (f32[512,128]{1,0:T(8,128)S(1)}, f32[512,128]{1,0:T(8,128)}, u32[]{:S(2)}) copy-start(f32[512,128]{1,0:T(8,128)} %fusion.76) | copy-start | bytes 786436
  189.1 3.6 %copy-start.16 = (f32[512,128]{1,0:T(8,128)S(1)}, f32[512,128]{1,0:T(8,128)}, u32[]{:S(2)}) copy-start(f32[512,128]{1,0:T(8,128)} %fusion.74) | copy-start | bytes 786436
  200.5 7.9 %copy-start.3 = (f32[1024,2,128]{0,2,1:T(8,128)S(1)}, f32[1024,2,128]{0,2,1:T(8,128)}, u32[]{:S(2)}) copy-start(f32[1024,2,128]{0,2,1:T(8,128)} %get-tuple-element.12) | copy-start | bytes 3145732
  200.5 7.9 %copy-start.24 = (f32[256]{0:T(256)S(1)}, f32[256]{0:T(256)}, u32[]{:S(2)}) copy-start(f32[256]{0:T(256)} %get-tuple-element.52) | copy-start | bytes 3076
  200.5 7.9 %copy-start.25 = (f32[256]{0:T(256)S(1)}, f32[256]{0:T(256)}, u32[]{:S(2)}) copy-start(f32[256]{0:T(256)} %get-tuple-element.53) | copy-start | bytes 3076
  202.3 13.5 %all-to-all-start.8 = ((bf16[16,1,2,2,2048]{4,3,2,1,0:T(2,128)(2,1)}), bf16[16,1,2,2,2048]{4,3,2,1,0:T(2,128)(2,1)S(1)}, u32[]{:S(2)}, u32[]{:S(2)}) async-start(bf16[16,1,2,2,2048]{4,3,2,1,0:T(2,128)(2,1)} %reshape.385), calls=%async_computation.8 | async-start | bytes 524288 | tf_op jit(solution)/shard_map/all_to_all | solution.py:182
  213.4 9.1 %copy-start.28 = (f32[128]{0:T(128)S(1)}, f32[128]{0:T(128)}, u32[]{:S(2)}) copy-start(f32[128]{0:T(128)} %get-tuple-element.5) | copy-start | bytes 1540
  213.4 141.8 %copy-start.27 = (s32[16]{0:T(128)S(1)}, s32[16]{0:T(128)}, u32[]{:S(2)}) copy-start(s32[16]{0:T(128)} %copy-done.26) | copy-start | bytes 196
  215.8 140.4 %all-to-all-start.6 = ((bf16[1,1024,3,256]{3,2,0,1:T(4,128)(2,1)}), bf16[1,1024,3,256]{3,2,0,1:T(4,128)(2,1)}, u32[]{:S(2)}, u32[]{:S(2)}) async-start(bf16[1,1024,3,256]{3,2,0,1:T(4,128)(2,1)} %copy.143), calls=%async_computation.6 | async-start | bytes 4194304 | tf_op jit(solution)/shard_map/all_to_all | solution.py:176
  (14 other events, 23.6 us)
where the time goes:
time: 364 us; the launch traced here: 361 us
  blocking collectives  132 us (36%)
  waiting for transfers between devices  63.6 us (17%)
  local copies, waits for them, and re-layouts  59.6 us (16%)
  starting transfers between devices  58.6 us (16%)
  other arithmetic  30.2 us (8%)
  matrix products  15.6 us (4%)
    psum x1, blocking collectives, on_device(): gain_total = lax.psum(gain_terms, ('fsdp', 'sp', 'enc'))  132 us
    all_to_all x1, waiting for transfers between devices, on_device(): lax.all_to_all(image_qkv, 'sp', split_axis=3, concat_axis=1, tiled=True)  39.8 us
    unnamed x68, local copies, waits for them, and re-layouts  14.9 us
    unnamed x1, other arithmetic  11.5 us
    all_to_all x1, starting transfers between devices, on_device(): lax.all_to_all(slot_flags, 'sp', split_axis=4, concat_axis=1, tiled=True)  10.3 us
    all_to_all x1, waiting for transfers between devices, on_device(): lax.all_to_all(grad_input, 'sp', split_axis=3, concat_axis=1, tiled=True)  8.68 us
    all_to_all x1, starting transfers between devices, on_device(): lax.all_to_all(lax.all_to_all(slot_flags, 'sp', split_axis=4, concat_axis...  8.58 us
    all_to_all x1, starting transfers between devices, on_device(): lax.all_to_all(lax.all_to_all(send_rows, 'sp', split_axis=4, concat_axis=...  8.12 us
  transfers between devices with their start and end apart: 9, of which 6 were waited for; matrix products, arithmetic and copies ran while one was open for 14% of the time, Pallas kernels for 0%

commit v1 on v0

v1 whole, which is shorter than its diff:
```python
import functools
import math

import jax
import jax.numpy as jnp
from jax import lax
from jax.experimental import pallas as pl
from jax.experimental.pallas import tpu as pltpu
from jax.sharding import PartitionSpec as P

EPSILON = 1e-06
CAP = 2
F32 = jnp.float32
BF16 = jnp.bfloat16
MESH = pl.DeviceIdType.MESH


def dot(a, b):
    return jnp.dot(a, b, preferred_element_type=F32)


def dot_nt(a, b):
    return lax.dot_general(a, b, (((1,), (1,)), ((), ())), preferred_element_type=F32)


def kernel(
    sizes,
    qkv,
    cot,
    txt,
    routes,
    q_gain,
    k_gain,
    t_gain,
    out_img,
    out_txt,
    out_gain,
    rows_in,
    grads_in,
    sends,
    sigma,
    sigmas,
    text_in,
    slots,
    text_keys,
    text_sends,
    slots_back,
    text_back,
    gain_own,
    gain_z,
    gain_e,
    gain_f,
    place_t,
    qn_t,
    unit_t,
    factor_t,
    g_t,
    keys,
    keys_t,
    values,
    values_t,
    weights,
    packs,
    dk_sum,
    dv_sum,
    q_term,
    kt_term,
    own_sem,
    own_head,
    own_back,
    sg_send,
    sg_recv,
    tx_send,
    tx_recv,
    fw_send,
    fw_recv,
    ct_send,
    ct_recv,
    bk_send,
    bk_recv,
    en_send,
    en_recv,
    eb_send,
    eb_recv,
    tb_send,
    tb_recv,
    gz_send,
    gz_recv,
    ge_send,
    ge_recv,
    gf_send,
    gf_recv,
):
    n_fs, n_sp, n_en = sizes
    fs, sp, en = lax.axis_index("fsdp"), lax.axis_index("sp"), lax.axis_index("enc")
    rows, width = cot.shape
    text_rows = txt.shape[1]
    hd = q_gain.shape[1]
    local = width // n_sp
    heads = local // hd
    seq = rows * n_sp
    per_enc = CAP * n_sp
    n_slots = per_enc * n_en
    n_text = text_rows * n_sp
    scale = hd ** (-0.5)
    z_steps = sorted(range(1, n_sp), key=lambda d: -min(d, n_sp - d))
    e_steps = list(range(1, n_en))
    f_steps = list(range(1, n_fs))

    def aligned(index, size):
        return pl.ds(pl.multiple_of(index * size, size), size)

    def on(axis, me, step, size):
        return {axis: lax.rem(me + step, size)}, lax.rem(me + step, size)

    barrier = pltpu.get_barrier_semaphore()
    for axis, me, steps, size in (
        ("sp", sp, z_steps, n_sp),
        ("enc", en, e_steps, n_en),
        ("fsdp", fs, f_steps, n_fs),
    ):
        for step in steps:
            pl.semaphore_signal(barrier, inc=1, device_id=on(axis, me, step, size)[0], device_id_type=MESH)

    def remote(src, dst, send, recv, device):
        return pltpu.make_async_remote_copy(
            src_ref=src, dst_ref=dst, send_sem=send, recv_sem=recv, device_id=device, device_id_type=MESH
        )

    def copy_sigma(i):
        device, _ = on("sp", sp, z_steps[i], n_sp)
        return remote(sigma, sigmas.at[aligned(sp, text_rows)], sg_send.at[i], sg_recv.at[i], device)

    def copy_text(i):
        device, peer = on("sp", sp, z_steps[i], n_sp)
        return remote(
            txt.at[:, :, aligned(peer, local)],
            text_in.at[:, aligned(sp, text_rows), :],
            tx_send.at[i],
            tx_recv.at[i],
            device,
        )

    def copy_rows(h, i):
        device, peer = on("sp", sp, z_steps[i], n_sp)
        return remote(
            qkv.at[:, :, aligned(peer * heads + h, hd)],
            rows_in.at[h, :, aligned(sp, rows), :],
            fw_send.at[h, i],
            fw_recv.at[h, i],
            device,
        )

    def copy_cot(h, i):
        device, peer = on("sp", sp, z_steps[i], n_sp)
        return remote(
            cot.at[:, aligned(peer * heads + h, hd)],
            grads_in.at[h, aligned(sp, rows), :],
            ct_send.at[h, i],
            ct_recv.at[h, i],
            device,
        )

    def copy_back(h, i):
        device, peer = on("sp", sp, z_steps[i], n_sp)
        return remote(
            sends.at[h, :, aligned(peer, rows), :],
            out_img.at[:, :, aligned(sp * heads + h, hd)],
            bk_send.at[h, i],
            bk_recv.at[h, i],
            device,
        )

    def copy_slots(i):
        device, peer = on("enc", en, e_steps[i], n_en)
        return remote(
            slots.at[aligned(peer, per_enc)],
            text_keys.at[aligned(en, per_enc)],
            en_send.at[i],
            en_recv.at[i],
            device,
        )

    def copy_slots_back(i):
        device, peer = on("enc", en, e_steps[i], n_en)
        return remote(
            text_sends.at[aligned(peer, per_enc)],
            slots_back.at[aligned(en, per_enc)],
            eb_send.at[i],
            eb_recv.at[i],
            device,
        )

    def copy_text_back(i):
        device, peer = on("sp", sp, z_steps[i], n_sp)
        return remote(
            text_back.at[:, aligned(peer, text_rows), :],
            out_txt.at[:, :, aligned(sp, local)],
            tb_send.at[i],
            tb_recv.at[i],
            device,
        )

    def copy_gain(i, level):
        axis, me, steps, size, own, dst, send, recv = (
            ("sp", sp, z_steps, n_sp, gain_own.at[0], gain_z, gz_send, gz_recv),
            ("enc", en, e_steps, n_en, gain_own.at[1], gain_e, ge_send, ge_recv),
            ("fsdp", fs, f_steps, n_fs, gain_own.at[2], gain_f, gf_send, gf_recv),
        )[level]
        device, _ = on(axis, me, steps[i], size)
        return remote(own, dst.at[me], send.at[i], recv.at[i], device)

    own_sigma = pltpu.make_async_copy(sigma, sigmas.at[aligned(sp, text_rows)], own_sem.at[0])
    own_text = pltpu.make_async_copy(
        txt.at[:, :, aligned(sp, local)], text_in.at[:, aligned(sp, text_rows), :], own_sem.at[1]
    )
    own_slots = pltpu.make_async_copy(
        slots.at[aligned(en, per_enc)], text_keys.at[aligned(en, per_enc)], own_sem.at[2]
    )
    own_slots_back = pltpu.make_async_copy(
        text_sends.at[aligned(en, per_enc)], slots_back.at[aligned(en, per_enc)], own_sem.at[3]
    )
    own_text_back = pltpu.make_async_copy(
        text_back.at[:, aligned(sp, text_rows), :], out_txt.at[:, :, aligned(sp, local)], own_sem.at[4]
    )

    def own_rows(h):
        return pltpu.make_async_copy(
            qkv.at[:, :, aligned(sp * heads + h, hd)], rows_in.at[h, :, aligned(sp, rows), :], own_head.at[0, h]
        )

    def own_cot(h):
        return pltpu.make_async_copy(
            cot.at[:, aligned(sp * heads + h, hd)], grads_in.at[h, aligned(sp, rows), :], own_head.at[1, h]
        )

    def own_image_back(h):
        return pltpu.make_async_copy(
            sends.at[h, :, aligned(sp, rows), :], out_img.at[:, :, aligned(sp * heads + h, hd)], own_back.at[h]
        )

    dest_lane = jnp.broadcast_to(routes[...].astype(F32), (text_rows, text_rows))
    row_at = lax.broadcasted_iota(jnp.int32, (text_rows, text_rows), 0)
    col_at = lax.broadcasted_iota(jnp.int32, (text_rows, text_rows), 1)
    dest_col = jnp.sum(jnp.where(row_at == col_at, dest_lane, 0.0), axis=1, keepdims=True)
    same = jnp.where((dest_col == dest_lane) & (col_at < row_at), 1.0, 0.0)
    rank = jnp.sum(same, axis=1, keepdims=True)
    shard_first = jnp.full((text_rows, 1), sp * CAP, jnp.int32).astype(F32)
    sigma[...] = jnp.broadcast_to(dest_col * per_enc + shard_first + rank, sigma.shape).astype(BF16)

    own_sigma.start()
    own_text.start()
    for h in range(heads):
        own_rows(h).start()
        own_cot(h).start()

    pl.semaphore_wait(barrier, len(z_steps) + len(e_steps) + len(f_steps))

    for i in range(len(z_steps)):
        copy_sigma(i).start()
        copy_text(i).start()
    for h in range(heads):
        for i in range(len(z_steps)):
            copy_rows(h, i).start()
            copy_cot(h, i).start()

    own_sigma.wait()
    own_text.wait()
    for i in range(len(z_steps)):
        copy_sigma(i).wait()
        copy_text(i).wait()
    slot_at = lax.broadcasted_iota(jnp.int32, (n_text, n_slots), 1).astype(F32)
    row_slot = jnp.concatenate([sigmas[...].astype(F32)] * (n_slots // sigma.shape[1]), axis=1)
    placed_t = jnp.where(row_slot == slot_at, 1.0, 0.0)
    place_t[...] = placed_t.astype(BF16)
    placed = placed_t.T
    for part in range(2):
        slots[:, part * local : (part + 1) * local] = dot(placed.astype(BF16), text_in[part]).astype(BF16)
    live_col = jnp.sum(placed, axis=1, keepdims=True)
    slots[:, 2 * local :] = jnp.broadcast_to(live_col, (n_slots, hd)).astype(BF16)
    own_slots.start()
    for i in range(len(e_steps)):
        copy_slots(i).start()
    own_slots.wait()
    for i in range(len(e_steps)):
        copy_slots(i).wait()

    chunk = 256
    q_chunk = weights.shape[1]
    n_image = seq // chunk
    key_parts = [(c * chunk, chunk, False) for c in range(n_image)] + [(seq, n_slots, True)]
    gain_col = jnp.broadcast_to(q_gain[...], (hd, hd)).T
    q_gain_t = jnp.concatenate([gain_col] * (q_chunk // hd), axis=1)

    def norm_rows(raw, gain):
        factor = lax.rsqrt(jnp.mean(raw * raw, axis=-1, keepdims=True) + EPSILON)
        unit = raw * factor
        return unit * gain, unit, factor

    def norm_rows_back(grad, unit, factor, gain):
        scaled = grad * gain
        inner = jnp.mean(scaled * unit, axis=-1, keepdims=True)
        return factor * (scaled - unit * inner)

    def one_head(h, carry):
        own_rows(h).wait()
        own_cot(h).wait()
        for i in range(len(z_steps)):
            copy_rows(h, i).wait_recv()
            copy_cot(h, i).wait_recv()

        def prepare(c, carry):
            at = aligned(c, chunk)
            raw_t = rows_in[h, 0, at, :].astype(F32).T
            factor = lax.rsqrt(jnp.mean(raw_t * raw_t, axis=0, keepdims=True) + EPSILON)
            unit = raw_t * factor
            unit_t[:, at] = unit
            factor_t[:, at] = factor
            qn_t[:, at] = (unit * q_gain_t[:, :chunk]).astype(BF16)
            g_t[:, at] = grads_in[h, at, :].astype(F32).T
            normed = norm_rows(rows_in[h, 1, at, :].astype(F32), k_gain[...])[0]
            keys[at, :] = normed.astype(BF16)
            keys_t[:, at] = normed.T.astype(BF16)
            value = rows_in[h, 2, at, :]
            values[at, :] = value
            values_t[:, at] = value.astype(F32).T.astype(BF16)
            return carry

        lax.fori_loop(0, n_image, prepare, 0)
        text_at = pl.ds(seq, n_slots)
        normed = norm_rows(text_keys[:, aligned(h, hd)].astype(F32), t_gain[...])[0]
        keys[text_at, :] = normed.astype(BF16)
        keys_t[:, text_at] = normed.T.astype(BF16)
        value = text_keys[:, aligned(heads + h, hd)]
        values[text_at, :] = value
        values_t[:, text_at] = value.astype(F32).T.astype(BF16)
        dk_sum[...] = jnp.zeros_like(dk_sum)
        dv_sum[...] = jnp.zeros_like(dv_sum)

        def queries(j, carry):
            at = aligned(j, q_chunk)
            qn = qn_t[:, at]
            total = jnp.zeros((1, q_chunk), F32)
            numer = jnp.zeros((hd, q_chunk), F32)
            for first, count, is_text in key_parts:
                part = pl.ds(first, count)
                weight = jnp.exp2(dot(keys[part, :], qn) * (scale * math.log2(math.e)))
                if is_text:
                    live = text_keys[:, 2 * local :].astype(F32)
                    weight = weight * jnp.concatenate([live] * (q_chunk // hd), axis=1)
                total += jnp.sum(weight, axis=0, keepdims=True)
                packed = weight.astype(BF16)
                weights[part, :] = weight
                packs[part, :] = packed
                numer += dot(values_t[:, part], packed)
            inverse = 1.0 / total
            scaled_wide = g_t[:, at] * inverse
            scaled = scaled_wide.astype(BF16)
            grad_total = -jnp.sum(scaled_wide * (numer * inverse), axis=0, keepdims=True)
            dq = jnp.zeros((hd, q_chunk), F32)
            for first, count, _ in key_parts:
                part = pl.ds(first, count)
                back = dot(values[part, :], scaled)
                tangent = ((back + grad_total) * weights[part, :] * scale).astype(BF16)
                dq += dot(keys_t[:, part], tangent)
                dk_sum[part, :] += dot_nt(tangent, qn)
                dv_sum[part, :] += dot_nt(packs[part, :], scaled)
            unit = unit_t[:, at]
            q_term[...] += dq * unit
            spread = dq * q_gain_t
            inner = jnp.mean(spread * unit, axis=0, keepdims=True)
            dx = factor_t[:, at] * (spread - unit * inner)
            sends[h, 0, at, :] = dx.T.astype(BF16)
            return carry

        lax.fori_loop(0, seq // q_chunk, queries, 0)

        def finish(c, carry):
            at = aligned(c, chunk)
            dk = dk_sum[at, :]
            _, unit, factor = norm_rows(rows_in[h, 1, at, :].astype(F32), k_gain[...])
            kt_term[0:1, :] += jnp.sum(dk * unit, axis=0, keepdims=True)
            sends[h, 1, at, :] = norm_rows_back(dk, unit, factor, k_gain[...]).astype(BF16)
            sends[h, 2, at, :] = dv_sum[at, :].astype(BF16)
            return carry

        lax.fori_loop(0, n_image, finish, 0)
        dk = dk_sum[text_at, :]
        _, unit, factor = norm_rows(text_keys[:, aligned(h, hd)].astype(F32), t_gain[...])
        kt_term[1:2, :] += jnp.sum(dk * unit, axis=0, keepdims=True)
        text_sends[:, aligned(h, hd)] = norm_rows_back(dk, unit, factor, t_gain[...]).astype(BF16)
        text_sends[:, aligned(heads + h, hd)] = dv_sum[text_at, :].astype(BF16)

        @pl.when(h == heads - 1)
        def _():
            gain_own[0, 0:1, :] = jnp.sum(q_term[...].T, axis=0, keepdims=True)
            gain_own[0, 1:3, :] = kt_term[0:2, :]
            gain_z[sp] = gain_own[0]
            for i in range(len(z_steps)):
                copy_gain(i, 0).start()
            own_slots_back.start()
            for i in range(len(e_steps)):
                copy_slots_back(i).start()

        for i in range(len(z_steps)):
            copy_back(h, i).start()
        own_image_back(h).start()
        return carry

    q_term[...] = jnp.zeros_like(q_term)
    kt_term[...] = jnp.zeros_like(kt_term)
    gain_own[...] = jnp.zeros_like(gain_own)
    lax.fori_loop(0, heads, one_head, 0)

    for i in range(len(z_steps)):
        copy_gain(i, 0).wait()
    gain_own[1] = jnp.sum(gain_z[...], axis=0)
    gain_e[en] = gain_own[1]
    for i in range(len(e_steps)):
        copy_gain(i, 1).start()
    own_slots_back.wait()
    for i in range(len(e_steps)):
        copy_slots_back(i).wait()
    for part in range(2):
        mine = slots_back[:, part * local : (part + 1) * local]
        text_back[part] = dot(place_t[...], mine).astype(BF16)
    own_text_back.start()
    for i in range(len(z_steps)):
        copy_text_back(i).start()
    for i in range(len(e_steps)):
        copy_gain(i, 1).wait()
    gain_own[2] = jnp.sum(gain_e[...], axis=0)
    gain_f[fs] = gain_own[2]
    for i in range(len(f_steps)):
        copy_gain(i, 2).start()
    for i in range(len(f_steps)):
        copy_gain(i, 2).wait()
    sample_count = n_fs * n_en
    scale_total = float(sample_count * seq * heads * n_sp) ** (-0.5)
    out_gain[...] = jnp.sum(gain_f[...], axis=0)[0:3, :] * scale_total

    for h in range(heads):
        for i in range(len(z_steps)):
            copy_rows(h, i).wait_send()
            copy_cot(h, i).wait_send()
            copy_back(h, i).wait()
        own_image_back(h).wait()
    own_text_back.wait()
    for i in range(len(z_steps)):
        copy_text_back(i).wait()


def on_device(sizes, image_qkv, cotangent, text_kv, routes, q_gain, k_gain, text_gain):
    n_fs, n_sp, n_en = sizes
    _, rows, _, width = image_qkv.shape
    text_rows = text_kv.shape[0]
    hd = q_gain.shape[0]
    local = width // n_sp
    heads = local // hd
    seq = rows * n_sp
    n_slots = CAP * n_sp * n_en
    n_text = text_rows * n_sp
    n_keys = seq + n_slots
    q_chunk = 256
    qkv = image_qkv[0].transpose(1, 0, 2)
    txt = text_kv.transpose(1, 0, 2)
    dma = pltpu.SemaphoreType.DMA
    z, e, f = n_sp - 1, n_en - 1, n_fs - 1
    any_spec = pl.BlockSpec(memory_space=pl.ANY)
    vmem_spec = pl.BlockSpec(memory_space=pltpu.VMEM)
    out_img, out_txt, out_gain = pl.pallas_call(
        functools.partial(kernel, sizes),
        out_shape=(
            jax.ShapeDtypeStruct((3, rows, width), BF16),
            jax.ShapeDtypeStruct((2, text_rows, width), BF16),
            jax.ShapeDtypeStruct((3, hd), F32),
        ),
        in_specs=[any_spec] * 3 + [vmem_spec] * 4,
        out_specs=(any_spec, any_spec, vmem_spec),
        scratch_shapes=[
            pltpu.VMEM((heads, 3, seq, hd), BF16),
            pltpu.VMEM((heads, seq, hd), BF16),
            pltpu.VMEM((heads, 3, seq, hd), BF16),
            pltpu.VMEM((text_rows, hd), BF16),
            pltpu.VMEM((n_text, hd), BF16),
            pltpu.VMEM((2, n_text, local), BF16),
            pltpu.VMEM((n_slots, 2 * local + hd), BF16),
            pltpu.VMEM((n_slots, 2 * local + hd), BF16),
            pltpu.VMEM((n_slots, 2 * local), BF16),
            pltpu.VMEM((n_slots, 2 * local), BF16),
            pltpu.VMEM((2, n_text, local), BF16),
            pltpu.VMEM((3, 8, hd), F32),
            pltpu.VMEM((n_sp, 8, hd), F32),
            pltpu.VMEM((n_en, 8, hd), F32),
            pltpu.VMEM((n_fs, 8, hd), F32),
            pltpu.VMEM((n_text, n_slots), BF16),
            pltpu.VMEM((hd, seq), BF16),
            pltpu.VMEM((hd, seq), F32),
            pltpu.VMEM((1, seq), F32),
            pltpu.VMEM((hd, seq), F32),
            pltpu.VMEM((n_keys, hd), BF16),
            pltpu.VMEM((hd, n_keys), BF16),
            pltpu.VMEM((n_keys, hd), BF16),
            pltpu.VMEM((hd, n_keys), BF16),
            pltpu.VMEM((n_keys, q_chunk), F32),
            pltpu.VMEM((n_keys, q_chunk), BF16),
            pltpu.VMEM((n_keys, hd), F32),
            pltpu.VMEM((n_keys, hd), F32),
            pltpu.VMEM((hd, q_chunk), F32),
            pltpu.VMEM((8, hd), F32),
            dma((5,)),
            dma((2, heads)),
            dma((heads,)),
        ]
        + [dma((z,))] * 4
        + [dma((heads, z))] * 6
        + [dma((e,))] * 4
        + [dma((z,))] * 4
        + [dma((e,))] * 2
        + [dma((f,))] * 2,
        compiler_params=pltpu.CompilerParams(
            collective_id=0, has_side_effects=True, vmem_limit_bytes=40 << 20
        ),
    )(
        qkv,
        cotangent[0],
        txt,
        routes.reshape(1, text_rows),
        q_gain.reshape(1, hd),
        k_gain.reshape(1, hd),
        text_gain.reshape(1, hd),
    )
    return out_img.transpose(1, 0, 2)[None], out_txt.transpose(1, 0, 2), out_gain


def solution(mesh):
    sizes = tuple(mesh.shape[axis] for axis in ("fsdp", "sp", "enc"))
    placed = (
        P(("fsdp", "enc"), "sp", None, None),
        P(("fsdp", "enc"), "sp", None),
        P(("fsdp", "sp", "enc"), None, None),
        P(("fsdp", "sp", "enc"), None),
        P(),
        P(),
        P(),
    )
    return jax.shard_map(
        functools.partial(on_device, sizes),
        mesh=mesh,
        in_specs=placed,
        out_specs=(P(("fsdp", "enc"), "sp", None, None), P(("fsdp", "sp", "enc"), None, None), P()),
        check_vma=False,
    )
```

time: 364 us -> 114 us (0.31)
  blocking collectives: 132 us -> 0 us
  Pallas kernels: 0 us -> 104 us
  waiting for transfers between devices: 63.6 us -> 0 us
  starting transfers between devices: 58.6 us -> 0 us
  local copies, waits for them, and re-layouts: 59.6 us -> 8.52 us
  other arithmetic: 30.2 us -> 0 us
  matrix products: 15.6 us -> 0 us
    psum x1 -> x0, blocking collectives: 132 us -> none  [on_device(): gain_total = lax.psum(gain_terms, ('fsdp', 'sp', 'enc'))]
    pallas_call x0 -> x1, Pallas kernels: none -> 104 us  [on_device(): pl.pallas_call(functools.partial(kernel, sizes), out_shape=(jax.ShapeDtyp...]
    all_to_all x9 -> x0, waiting for transfers between devices: 63.6 us -> none  [the longest x1 39.8 us: on_device(): lax.all_to_all(image_qkv, 'sp', split_axis=3, concat_axis=1, tiled=True)]
    all_to_all x9 -> x0, starting transfers between devices: 58.6 us -> none  [the longest x1 10.3 us: on_device(): lax.all_to_all(slot_flags, 'sp', split_axis=4, concat_axis=1, tiled=True)]
    all_to_all x12 -> x0, local copies, waits for them, and re-layouts: 19.6 us -> none  [the longest x2 6.56 us: on_device(): lax.all_to_all(image_qkv, 'sp', split_axis=3, concat_axis=1, tiled=True)]
    dot_general x26 -> x0, matrix products: 15.6 us -> none  [the longest x4 4.85 us: attend_block(): grad_query = jnp.dot(tangent, key_rows, preferred_element_type=jnp.float32)]
    another operation x13 -> x0, local copies, waits for them, and re-layouts: 14.3 us -> none  [the longest x2 3.86 us: on_device(): jnp.stack(dq_list, axis=1)]
    unnamed x1 -> x0, other arithmetic: 11.5 us -> none
  transfers between devices with their start and end apart: 9 -> 0, of which waited for: 6 -> 0; matrix products, arithmetic and copies ran while one was open for 14% -> 0% of each run, Pallas kernels for 0% -> 0%
where the time goes in v1:
time: 114 us; the launch traced here: 113 us
  Pallas kernels  104 us (91%)
  local copies, waits for them, and re-layouts  8.52 us (7%)
    pallas_call x1, Pallas kernels, on_device(): pl.pallas_call(functools.partial(kernel, sizes), out_shape=(jax.ShapeDtyp...  104 us
    unnamed x16, local copies, waits for them, and re-layouts  8.52 us

profile of v1, /device:TPU:6, one launch (start us, length us, event | category | flops | bytes accessed | tf_op | source)
XLA Modules:
  0.0 113.4 jit_solution(14443055286727817343)
XLA Ops:
  0.6 0.9 copy.13
  1.6 0.0 copy-start
  1.6 1.4 %copy-done = bf16[1,128,3,2048]{3,1,2,0:T(8,128)(2,1)S(1)} copy-done((bf16[1,128,3,2048]{3,1,2,0:T(8,128)(2,1)S(1)}, bf16[1,128,3,2048]{3,1,2,0:T(8,128)(2,1)}, u32[]{:S(2)}) %copy-start) | copy-done | bytes 1572888
  3.0 0.0 copy-start.1
  3.0 1.0 copy-done.1
  4.0 0.0 copy-start.2
  4.0 0.7 copy-done.2
  4.7 0.0 copy-start.3
  4.7 0.7 copy-done.3
  5.3 0.0 copy-start.4
  5.3 0.7 copy-done.4
  6.0 0.0 copy-start.5
  6.0 0.7 copy-done.5
  6.7 104.2 %shard_map.94 = (bf16[3,128,2048]{2,1,0:T(8,128)(2,1)S(1)}, bf16[2,16,2048]{2,1,0:T(8,128)(2,1)S(1)}, f32[3,128]{1,0:T(4,128)S(1)}) custom-call(bf16[3,128,2048]{2,1,0:T(8,128)(2,1)S(1)} %bitcast.15, bf16[128,2048]{1,0:T(8,128)(2,1)S(1)} %bitcast.17, bf16[2,16,2048]{2,1,0:T(8,128)(2,1)S(1)} %bitcast.18, s32[1,16]{1,0:T(1,128)S(1)} %bitcast.20, ...), custom_call_target="tpu_custom_call" | custom-call | tf_op jit(solution)/shard_map/pallas_call | solution.py:471
  110.9 0.8 copy.11
  111.7 1.1 %copy.16 = bf16[1,128,3,2048]{3,1,2,0:T(8,128)(2,1)} copy(bf16[1,128,3,2048]{3,1,2,0:T(8,128)(2,1)S(1)} %bitcast.16) | data formatting | bytes 3145728
  112.8 0.6 copy.17
Async XLA Ops:
  1.6 1.4 %copy-start = (bf16[1,128,3,2048]{3,1,2,0:T(8,128)(2,1)S(1)}, bf16[1,128,3,2048]{3,1,2,0:T(8,128)(2,1)}, u32[]{:S(2)}) copy-start(bf16[1,128,3,2048]{3,1,2,0:T(8,128)(2,1)} %param.7) | copy-start | bytes 4718596
  3.0 1.0 copy-start.1
  4.0 0.7 copy-start.2
  4.7 0.7 copy-start.3
  5.3 0.7 copy-start.4
  6.0 0.7 copy-start.5

commit v2 on v1

--- a/solution.py
+++ b/solution.py
@@ -28,18 +28,19 @@
     qkv,
     cot,
     txt,
-    routes,
-    q_gain,
-    k_gain,
-    t_gain,
+    routes_hbm,
+    q_gain_hbm,
+    k_gain_hbm,
+    t_gain_hbm,
     out_img,
     out_txt,
     out_gain,
     rows_in,
     grads_in,
     sends,
-    sigma,
-    sigmas,
+    routes,
+    routes_in,
+    gains,
     text_in,
     slots,
     text_keys,
@@ -90,12 +91,15 @@
     ge_recv,
     gf_send,
     gf_recv,
+    above,
+    line,
 ):
     n_fs, n_sp, n_en = sizes
     fs, sp, en = lax.axis_index("fsdp"), lax.axis_index("sp"), lax.axis_index("enc")
     rows, width = cot.shape
-    text_rows = txt.shape[1]
-    hd = q_gain.shape[1]
+    text_rows = txt.shape[0]
+    hd = gains.shape[2]
+    q_gain, k_gain, t_gain = gains.at[0], gains.at[1], gains.at[2]
     local = width // n_sp
     heads = local // hd
     seq = rows * n_sp
@@ -113,29 +117,37 @@
     def on(axis, me, step, size):
         return {axis: lax.rem(me + step, size)}, lax.rem(me + step, size)
 
+    layer = [("enc", en, step, n_en) for step in e_steps] + [("fsdp", fs, step, n_fs) for step in f_steps]
     barrier = pltpu.get_barrier_semaphore()
-    for axis, me, steps, size in (
-        ("sp", sp, z_steps, n_sp),
-        ("enc", en, e_steps, n_en),
-        ("fsdp", fs, f_steps, n_fs),
-    ):
-        for step in steps:
-            pl.semaphore_signal(barrier, inc=1, device_id=on(axis, me, step, size)[0], device_id_type=MESH)
+
+    def greet(sem, axis, me, step, size):
+        pl.semaphore_signal(sem, inc=1, device_id=on(axis, me, step, size)[0], device_id_type=MESH)
+
+    for step in range(1, n_sp):
+
+        @pl.when(sp + step < n_sp)
+        def _():
+            greet(barrier, "sp", sp, step, n_sp)
+
+    @pl.when(sp == 0)
+    def _():
+        for peer in layer:
+            greet(barrier, *peer)
 
     def remote(src, dst, send, recv, device):
         return pltpu.make_async_remote_copy(
             src_ref=src, dst_ref=dst, send_sem=send, recv_sem=recv, device_id=device, device_id_type=MESH
         )
 
-    def copy_sigma(i):
+    def copy_routes(i):
         device, _ = on("sp", sp, z_steps[i], n_sp)
-        return remote(sigma, sigmas.at[aligned(sp, text_rows)], sg_send.at[i], sg_recv.at[i], device)
+        return remote(routes, routes_in.at[sp], sg_send.at[i], sg_recv.at[i], device)
 
     def copy_text(i):
         device, peer = on("sp", sp, z_steps[i], n_sp)
         return remote(
             txt.at[:, :, aligned(peer, local)],
-            text_in.at[:, aligned(sp, text_rows), :],
+            text_in.at[aligned(sp, text_rows)],
             tx_send.at[i],
             tx_recv.at[i],
             device,
@@ -194,7 +206,7 @@
     def copy_text_back(i):
         device, peer = on("sp", sp, z_steps[i], n_sp)
         return remote(
-            text_back.at[:, aligned(peer, text_rows), :],
+            text_back.at[aligned(peer, text_rows)],
             out_txt.at[:, :, aligned(sp, local)],
             tb_send.at[i],
             tb_recv.at[i],
@@ -210,9 +222,12 @@
         device, _ = on(axis, me, steps[i], size)
         return remote(own, dst.at[me], send.at[i], recv.at[i], device)
 
-    own_sigma = pltpu.make_async_copy(sigma, sigmas.at[aligned(sp, text_rows)], own_sem.at[0])
+    fetches = [pltpu.make_async_copy(routes_hbm, routes, own_sem.at[0])] + [
+        pltpu.make_async_copy(src, gains.at[n], own_sem.at[5 + n])
+        for n, src in enumerate((q_gain_hbm, k_gain_hbm, t_gain_hbm))
+    ]
     own_text = pltpu.make_async_copy(
-        txt.at[:, :, aligned(sp, local)], text_in.at[:, aligned(sp, text_rows), :], own_sem.at[1]
+        txt.at[:, :, aligned(sp, local)], text_in.at[aligned(sp, text_rows)], own_sem.at[1]
     )
     own_slots = pltpu.make_async_copy(
         slots.at[aligned(en, per_enc)], text_keys.at[aligned(en, per_enc)], own_sem.at[2]
@@ -221,7 +236,7 @@
         text_sends.at[aligned(en, per_enc)], slots_back.at[aligned(en, per_enc)], own_sem.at[3]
     )
     own_text_back = pltpu.make_async_copy(
-        text_back.at[:, aligned(sp, text_rows), :], out_txt.at[:, :, aligned(sp, local)], own_sem.at[4]
+        text_back.at[aligned(sp, text_rows)], out_txt.at[:, :, aligned(sp, local)], own_sem.at[4]
     )
 
     def own_rows(h):
@@ -239,43 +254,93 @@
             sends.at[h, :, aligned(sp, rows), :], out_img.at[:, :, aligned(sp * heads + h, hd)], own_back.at[h]
         )
 
-    dest_lane = jnp.broadcast_to(routes[...].astype(F32), (text_rows, text_rows))
-    row_at = lax.broadcasted_iota(jnp.int32, (text_rows, text_rows), 0)
-    col_at = lax.broadcasted_iota(jnp.int32, (text_rows, text_rows), 1)
-    dest_col = jnp.sum(jnp.where(row_at == col_at, dest_lane, 0.0), axis=1, keepdims=True)
-    same = jnp.where((dest_col == dest_lane) & (col_at < row_at), 1.0, 0.0)
-    rank = jnp.sum(same, axis=1, keepdims=True)
-    shard_first = jnp.full((text_rows, 1), sp * CAP, jnp.int32).astype(F32)
-    sigma[...] = jnp.broadcast_to(dest_col * per_enc + shard_first + rank, sigma.shape).astype(BF16)
-
-    own_sigma.start()
+    for fetch in fetches:
+        fetch.start()
     own_text.start()
     for h in range(heads):
         own_rows(h).start()
         own_cot(h).start()
 
-    pl.semaphore_wait(barrier, len(z_steps) + len(e_steps) + len(f_steps))
+    for fetch in fetches:
+        fetch.wait()
+    routes_in[sp] = routes[...]
+    pl.semaphore_wait(barrier, jnp.where(sp == 0, len(layer), sp))
+
+    def first_sends(step):
+        i = z_steps.index(step)
+        copy_routes(i).start()
+        copy_text(i).start()
+        copy_rows(0, i).start()
+        copy_cot(0, i).start()
+
+    for step in range(1, n_sp):
+
+        @pl.when(sp + step >= n_sp)
+        def _():
+            greet(above.at[n_sp - step], "sp", sp, step, n_sp)
+
+    def text_sends_to(step):
+        i = z_steps.index(step)
+        copy_routes(i).start()
+        copy_text(i).start()
+
+    for step in z_steps:
+
+        @pl.when(sp + step >= n_sp)
+        def _():
+            text_sends_to(step)
+
+    for step in range(1, n_sp):
+
+        @pl.when(sp + step < n_sp)
+        def _():
+            pl.semaphore_wait(above.at[step], 1)
+            text_sends_to(step)
 
     for i in range(len(z_steps)):
-        copy_sigma(i).start()
-        copy_text(i).start()
-    for h in range(heads):
+        copy_rows(0, i).start()
+        copy_cot(0, i).start()
+
+    for h in range(1, heads):
         for i in range(len(z_steps)):
             copy_rows(h, i).start()
             copy_cot(h, i).start()
 
-    own_sigma.wait()
+    @pl.when(sp == 0)
+    def _():
+        for peer in layer:
+            greet(line, *peer)
+        pl.semaphore_wait(line, len(layer))
+        for step in range(1, n_sp):
+            greet(line, "sp", sp, step, n_sp)
+
+    @pl.when(sp > 0)
+    def _():
+        pl.semaphore_wait(line, 1)
+
     own_text.wait()
     for i in range(len(z_steps)):
-        copy_sigma(i).wait()
+        copy_routes(i).wait()
         copy_text(i).wait()
-    slot_at = lax.broadcasted_iota(jnp.int32, (n_text, n_slots), 1).astype(F32)
-    row_slot = jnp.concatenate([sigmas[...].astype(F32)] * (n_slots // sigma.shape[1]), axis=1)
-    placed_t = jnp.where(row_slot == slot_at, 1.0, 0.0)
+    row_at = lax.broadcasted_iota(jnp.int32, (text_rows, text_rows), 0)
+    col_at = lax.broadcasted_iota(jnp.int32, (text_rows, text_rows), 1)
+    slot_at = lax.broadcasted_iota(jnp.int32, (text_rows, n_slots), 1).astype(F32)
+    placed_parts = []
+    for shard in range(n_sp):
+        dest_lane = jnp.broadcast_to(routes_in[shard].astype(F32), (text_rows, text_rows))
+        dest_col = jnp.sum(jnp.where(row_at == col_at, dest_lane, 0.0), axis=1, keepdims=True)
+        same = jnp.where((dest_col == dest_lane) & (col_at < row_at), 1.0, 0.0)
+        rank = jnp.sum(same, axis=1, keepdims=True)
+        slot = dest_col * per_enc + (shard * CAP) + rank
+        placed_parts.append(jnp.where(slot == slot_at, 1.0, 0.0))
+    placed_t = jnp.concatenate(placed_parts, axis=0)
     place_t[...] = placed_t.astype(BF16)
     placed = placed_t.T
+    arrived = text_in[...].astype(F32)
     for part in range(2):
-        slots[:, part * local : (part + 1) * local] = dot(placed.astype(BF16), text_in[part]).astype(BF16)
+        slots[:, part * local : (part + 1) * local] = dot(
+            placed.astype(BF16), arrived[:, part, :].astype(BF16)
+        ).astype(BF16)
     live_col = jnp.sum(placed, axis=1, keepdims=True)
     slots[:, 2 * local :] = jnp.broadcast_to(live_col, (n_slots, hd)).astype(BF16)
     own_slots.start()
@@ -421,9 +486,8 @@
     own_slots_back.wait()
     for i in range(len(e_steps)):
         copy_slots_back(i).wait()
-    for part in range(2):
-        mine = slots_back[:, part * local : (part + 1) * local]
-        text_back[part] = dot(place_t[...], mine).astype(BF16)
+    mine = [dot(place_t[...], slots_back[:, part * local : (part + 1) * local]) for part in range(2)]
+    text_back[...] = jnp.stack(mine, axis=1).astype(BF16)
     own_text_back.start()
     for i in range(len(z_steps)):
         copy_text_back(i).start()
@@ -450,6 +514,21 @@
         copy_text_back(i).wait()
 
 
+def write_out(img, txt, gain, out_img, out_txt, out_gain, sems):
+    pieces = 4
+    rows = img.shape[1] // pieces
+    pairs = [
+        (img.at[t, p * rows : (p + 1) * rows], out_img.at[t, p * rows : (p + 1) * rows])
+        for t in range(3)
+        for p in range(pieces)
+    ] + [(txt, out_txt), (gain, out_gain)]
+    copies = [pltpu.make_async_copy(src, dst, sems.at[n]) for n, (src, dst) in enumerate(pairs)]
+    for copy in copies:
+        copy.start()
+    for copy in copies:
+        copy.wait()
+
+
 def on_device(sizes, image_qkv, cotangent, text_kv, routes, q_gain, k_gain, text_gain):
     n_fs, n_sp, n_en = sizes
     _, rows, _, width = image_qkv.shape
@@ -463,32 +542,33 @@
     n_keys = seq + n_slots
     q_chunk = 256
     qkv = image_qkv[0].transpose(1, 0, 2)
-    txt = text_kv.transpose(1, 0, 2)
     dma = pltpu.SemaphoreType.DMA
     z, e, f = n_sp - 1, n_en - 1, n_fs - 1
     any_spec = pl.BlockSpec(memory_space=pl.ANY)
+    hbm_spec = pl.BlockSpec(memory_space=pltpu.HBM)
     vmem_spec = pl.BlockSpec(memory_space=pltpu.VMEM)
     out_img, out_txt, out_gain = pl.pallas_call(
         functools.partial(kernel, sizes),
         out_shape=(
-            jax.ShapeDtypeStruct((3, rows, width), BF16),
-            jax.ShapeDtypeStruct((2, text_rows, width), BF16),
-            jax.ShapeDtypeStruct((3, hd), F32),
+            pltpu.VMEM((3, rows, width), BF16),
+            pltpu.VMEM((text_rows, 2, width), BF16),
+            pltpu.VMEM((3, hd), F32),
         ),
-        in_specs=[any_spec] * 3 + [vmem_spec] * 4,
+        in_specs=[hbm_spec] * 7,
         out_specs=(any_spec, any_spec, vmem_spec),
         scratch_shapes=[
             pltpu.VMEM((heads, 3, seq, hd), BF16),
             pltpu.VMEM((heads, seq, hd), BF16),
             pltpu.VMEM((heads, 3, seq, hd), BF16),
-            pltpu.VMEM((text_rows, hd), BF16),
-            pltpu.VMEM((n_text, hd), BF16),
-            pltpu.VMEM((2, n_text, local), BF16),
+            pltpu.VMEM((1, text_rows), jnp.int32),
+            pltpu.VMEM((n_sp, 1, text_rows), jnp.int32),
+            pltpu.VMEM((3, 1, hd), F32),
+            pltpu.VMEM((n_text, 2, local), BF16),
             pltpu.VMEM((n_slots, 2 * local + hd), BF16),
             pltpu.VMEM((n_slots, 2 * local + hd), BF16),
             pltpu.VMEM((n_slots, 2 * local), BF16),
             pltpu.VMEM((n_slots, 2 * local), BF16),
-            pltpu.VMEM((2, n_text, local), BF16),
+            pltpu.VMEM((n_text, 2, local), BF16),
             pltpu.VMEM((3, 8, hd), F32),
             pltpu.VMEM((n_sp, 8, hd), F32),
             pltpu.VMEM((n_en, 8, hd), F32),
@@ -508,7 +588,7 @@
             pltpu.VMEM((n_keys, hd), F32),
             pltpu.VMEM((hd, q_chunk), F32),
             pltpu.VMEM((8, hd), F32),
-            dma((5,)),
+            dma((8,)),
             dma((2, heads)),
             dma((heads,)),
         ]
@@ -517,20 +597,34 @@
         + [dma((e,))] * 4
         + [dma((z,))] * 4
         + [dma((e,))] * 2
-        + [dma((f,))] * 2,
+        + [dma((f,))] * 2
+        + [pltpu.SemaphoreType.REGULAR((n_sp,)), pltpu.SemaphoreType.REGULAR],
         compiler_params=pltpu.CompilerParams(
             collective_id=0, has_side_effects=True, vmem_limit_bytes=40 << 20
         ),
     )(
-        qkv,
-        cotangent[0],
-        txt,
-        routes.reshape(1, text_rows),
-        q_gain.reshape(1, hd),
-        k_gain.reshape(1, hd),
-        text_gain.reshape(1, hd),
+        *(
+            pltpu.with_memory_space_constraint(operand, pltpu.HBM)
+            for operand in (
+                qkv,
+                cotangent[0],
+                text_kv,
+                routes.reshape(1, text_rows),
+                q_gain.reshape(1, hd),
+                k_gain.reshape(1, hd),
+                text_gain.reshape(1, hd),
+            )
+        )
     )
-    return out_img.transpose(1, 0, 2)[None], out_txt.transpose(1, 0, 2), out_gain
+    results = (out_img, out_txt, out_gain)
+    out_img, out_txt, out_gain = pl.pallas_call(
+        write_out,
+        out_shape=tuple(jax.ShapeDtypeStruct(r.shape, r.dtype) for r in results),
+        in_specs=[vmem_spec] * 3,
+        out_specs=(hbm_spec,) * 3,
+        scratch_shapes=[dma((14,))],
+    )(*(pltpu.with_memory_space_constraint(result, pltpu.VMEM) for result in results))
+    return out_img.transpose(1, 0, 2)[None], out_txt, out_gain
 
 
 def solution(mesh):

time: 114 us -> 102 us (0.89)
  local copies, waits for them, and re-layouts: 8.52 us -> 0 us
  Pallas kernels: 104 us -> 100 us
    unnamed x16 -> x0, local copies, waits for them, and re-layouts: 8.52 us -> none
    pallas_call x1 -> x2, Pallas kernels: 104 us -> 100 us  [the longest x1 99 us: on_device(): pl.pallas_call(functools.partial(kernel, sizes), out_shape=(pltpu.VMEM((3...]
where the time goes in v2:
time: 102 us; the launch traced here: 101 us
  Pallas kernels  100 us (98%)
    pallas_call x1, Pallas kernels, on_device(): pl.pallas_call(functools.partial(kernel, sizes), out_shape=(pltpu.VMEM((3...  99 us

profile of v2, /device:TPU:6, one launch (start us, length us, event | category | flops | bytes accessed | tf_op | source)
XLA Modules:
  0.0 100.9 jit_solution(157056216251088398)
XLA Ops:
  0.6 99.0 %shard_map.94 = (bf16[3,128,2048]{2,1,0:T(8,128)(2,1)S(1)}, bf16[16,2,2048]{2,1,0:T(2,128)(2,1)S(1)}, f32[3,128]{1,0:T(4,128)S(1)}) custom-call(bf16[3,128,2048]{2,1,0:T(8,128)(2,1)} %bitcast.11, bf16[128,2048]{1,0:T(8,128)(2,1)} %bitcast.12, bf16[16,2,2048]{2,1,0:T(2,128)(2,1)} %txt.1, s32[1,16]{1,0:T(1,128)} %bitcast.13, f32[1,128]{1,0:T(1,128)} %bitcast.14, ...), custom_call_target="tpu_custom_call" | custom-call | tf_op jit(solution)/shard_map/pallas_call | solution.py:550
  99.6 1.3 %shard_map.95 = (bf16[3,128,2048]{2,1,0:T(8,128)(2,1)}, bf16[16,2,2048]{2,1,0:T(2,128)(2,1)}, f32[3,128]{1,0:T(4,128)}) custom-call(bf16[3,128,2048]{2,1,0:T(8,128)(2,1)S(1)} %get-tuple-element.9.img, bf16[16,2,2048]{2,1,0:T(2,128)(2,1)S(1)} %get-tuple-element.10.txt, f32[3,128]{1,0:T(4,128)S(1)} %get-tuple-element.11.gain), custom_call_target="tpu_custom_call" | custom-call | tf_op jit(solution)/shard_map/pallas_call | solution.py:620

commit v3 on v2

--- a/solution.py
+++ b/solution.py
@@ -38,7 +38,6 @@
     rows_in,
     grads_in,
     sends,
-    routes,
     routes_in,
     gains,
     text_in,
@@ -107,7 +106,7 @@
     n_slots = per_enc * n_en
     n_text = text_rows * n_sp
     scale = hd ** (-0.5)
-    z_steps = sorted(range(1, n_sp), key=lambda d: -min(d, n_sp - d))
+    z_steps = sorted(range(1, n_sp), key=lambda d: min(d, n_sp - d))
     e_steps = list(range(1, n_en))
     f_steps = list(range(1, n_fs))
 
@@ -141,7 +140,7 @@
 
     def copy_routes(i):
         device, _ = on("sp", sp, z_steps[i], n_sp)
-        return remote(routes, routes_in.at[sp], sg_send.at[i], sg_recv.at[i], device)
+        return remote(routes_hbm, routes_in.at[sp], sg_send.at[i], sg_recv.at[i], device)
 
     def copy_text(i):
         device, peer = on("sp", sp, z_steps[i], n_sp)
@@ -222,7 +221,7 @@
         device, _ = on(axis, me, steps[i], size)
         return remote(own, dst.at[me], send.at[i], recv.at[i], device)
 
-    fetches = [pltpu.make_async_copy(routes_hbm, routes, own_sem.at[0])] + [
+    fetches = [pltpu.make_async_copy(routes_hbm, routes_in.at[sp], own_sem.at[0])] + [
         pltpu.make_async_copy(src, gains.at[n], own_sem.at[5 + n])
         for n, src in enumerate((q_gain_hbm, k_gain_hbm, t_gain_hbm))
     ]
@@ -254,6 +253,14 @@
             sends.at[h, :, aligned(sp, rows), :], out_img.at[:, :, aligned(sp * heads + h, hd)], own_back.at[h]
         )
 
+    pl.semaphore_wait(barrier, jnp.where(sp == 0, len(layer), sp))
+
+    for step in range(1, n_sp):
+
+        @pl.when(sp + step >= n_sp)
+        def _():
+            greet(above.at[n_sp - step], "sp", sp, step, n_sp)
+
     for fetch in fetches:
         fetch.start()
     own_text.start()
@@ -261,45 +268,43 @@
         own_rows(h).start()
         own_cot(h).start()
 
-    for fetch in fetches:
-        fetch.wait()
-    routes_in[sp] = routes[...]
-    pl.semaphore_wait(barrier, jnp.where(sp == 0, len(layer), sp))
-
-    def first_sends(step):
-        i = z_steps.index(step)
-        copy_routes(i).start()
-        copy_text(i).start()
-        copy_rows(0, i).start()
-        copy_cot(0, i).start()
-
-    for step in range(1, n_sp):
-
-        @pl.when(sp + step >= n_sp)
-        def _():
-            greet(above.at[n_sp - step], "sp", sp, step, n_sp)
-
     def text_sends_to(step):
         i = z_steps.index(step)
         copy_routes(i).start()
         copy_text(i).start()
 
+    def head_sends_to(step):
+        i = z_steps.index(step)
+        copy_rows(0, i).start()
+        copy_cot(0, i).start()
+
     for step in z_steps:
 
         @pl.when(sp + step >= n_sp)
         def _():
             text_sends_to(step)
 
-    for step in range(1, n_sp):
-
-        @pl.when(sp + step < n_sp)
+    for step in range(1, n_sp - 1):
+
+        @pl.when(sp + step < n_sp - 1)
         def _():
             pl.semaphore_wait(above.at[step], 1)
             text_sends_to(step)
 
-    for i in range(len(z_steps)):
-        copy_rows(0, i).start()
-        copy_cot(0, i).start()
+    for step in z_steps:
+
+        @pl.when(sp + step != n_sp - 1)
+        def _():
+            head_sends_to(step)
+
+    for step in range(1, n_sp):
+
+        @pl.when(sp + step == n_sp - 1)
+        def _():
+            pl.semaphore_wait(above.at[step], 1)
+            text_sends_to(step)
+            head_sends_to(step)
+
 
     for h in range(1, heads):
         for i in range(len(z_steps)):
@@ -319,6 +324,8 @@
         pl.semaphore_wait(line, 1)
 
     own_text.wait()
+    for fetch in fetches:
+        fetch.wait()
     for i in range(len(z_steps)):
         copy_routes(i).wait()
         copy_text(i).wait()
@@ -560,7 +567,6 @@
             pltpu.VMEM((heads, 3, seq, hd), BF16),
             pltpu.VMEM((heads, seq, hd), BF16),
             pltpu.VMEM((heads, 3, seq, hd), BF16),
-            pltpu.VMEM((1, text_rows), jnp.int32),
             pltpu.VMEM((n_sp, 1, text_rows), jnp.int32),
             pltpu.VMEM((3, 1, hd), F32),
             pltpu.VMEM((n_text, 2, local), BF16),

time: 102 us -> 100 us (0.980); the launches traced: 101 us -> 99.9 us
  no operation moved by 1% of the time
where the time goes in v3:
time: 100 us; the launch traced here: 99.9 us
  Pallas kernels  99.3 us (99%)
    pallas_call x1, Pallas kernels, on_device(): pl.pallas_call(functools.partial(kernel, sizes), out_shape=(pltpu.VMEM((3...  98 us

profile of v3, /device:TPU:6, one launch (start us, length us, event | category | flops | bytes accessed | tf_op | source)
XLA Modules:
  0.0 99.9 jit_solution(13743040746453297153)
XLA Ops:
  0.6 98.0 %shard_map.94 = (bf16[3,128,2048]{2,1,0:T(8,128)(2,1)S(1)}, bf16[16,2,2048]{2,1,0:T(2,128)(2,1)S(1)}, f32[3,128]{1,0:T(4,128)S(1)}) custom-call(bf16[3,128,2048]{2,1,0:T(8,128)(2,1)} %bitcast.11, bf16[128,2048]{1,0:T(8,128)(2,1)} %bitcast.12, bf16[16,2,2048]{2,1,0:T(2,128)(2,1)} %txt.1, s32[1,16]{1,0:T(1,128)} %bitcast.13, f32[1,128]{1,0:T(1,128)} %bitcast.14, ...), custom_call_target="tpu_custom_call" | custom-call | tf_op jit(solution)/shard_map/pallas_call | solution.py:557
  98.6 1.3 %shard_map.95 = (bf16[3,128,2048]{2,1,0:T(8,128)(2,1)}, bf16[16,2,2048]{2,1,0:T(2,128)(2,1)}, f32[3,128]{1,0:T(4,128)}) custom-call(bf16[3,128,2048]{2,1,0:T(8,128)(2,1)S(1)} %get-tuple-element.9.img, bf16[16,2,2048]{2,1,0:T(2,128)(2,1)S(1)} %get-tuple-element.10.txt, f32[3,128]{1,0:T(4,128)S(1)} %get-tuple-element.11.gain), custom_call_target="tpu_custom_call" | custom-call | tf_op jit(solution)/shard_map/pallas_call | solution.py:626

commit v4 on v3

--- a/solution.py
+++ b/solution.py
@@ -465,8 +465,9 @@
 
         @pl.when(h == heads - 1)
         def _():
-            gain_own[0, 0:1, :] = jnp.sum(q_term[...].T, axis=0, keepdims=True)
-            gain_own[0, 1:3, :] = kt_term[0:2, :]
+            gain_own[0, :, 0:hd] = jnp.sum(q_term[...].T, axis=0, keepdims=True)
+            gain_own[0, :, hd : 2 * hd] = kt_term[0:1, :]
+            gain_own[0, :, 2 * hd : 3 * hd] = kt_term[1:2, :]
             gain_z[sp] = gain_own[0]
             for i in range(len(z_steps)):
                 copy_gain(i, 0).start()
@@ -474,14 +475,13 @@
             for i in range(len(e_steps)):
                 copy_slots_back(i).start()
 
-        for i in range(len(z_steps)):
+        for i in (0, 1, 6, 2, 3, 4, 5):
             copy_back(h, i).start()
         own_image_back(h).start()
         return carry
 
     q_term[...] = jnp.zeros_like(q_term)
     kt_term[...] = jnp.zeros_like(kt_term)
-    gain_own[...] = jnp.zeros_like(gain_own)
     lax.fori_loop(0, heads, one_head, 0)
 
     for i in range(len(z_steps)):
@@ -508,7 +508,9 @@
         copy_gain(i, 2).wait()
     sample_count = n_fs * n_en
     scale_total = float(sample_count * seq * heads * n_sp) ** (-0.5)
-    out_gain[...] = jnp.sum(gain_f[...], axis=0)[0:3, :] * scale_total
+    total_gain = jnp.sum(gain_f[...], axis=0) * scale_total
+    for n in range(3):
+        out_gain[n : n + 1, :] = total_gain[:, n * hd : (n + 1) * hd]
 
     for h in range(heads):
         for i in range(len(z_steps)):
@@ -575,10 +577,10 @@
             pltpu.VMEM((n_slots, 2 * local), BF16),
             pltpu.VMEM((n_slots, 2 * local), BF16),
             pltpu.VMEM((n_text, 2, local), BF16),
-            pltpu.VMEM((3, 8, hd), F32),
-            pltpu.VMEM((n_sp, 8, hd), F32),
-            pltpu.VMEM((n_en, 8, hd), F32),
-            pltpu.VMEM((n_fs, 8, hd), F32),
+            pltpu.VMEM((3, 1, 3 * hd), F32),
+            pltpu.VMEM((n_sp, 1, 3 * hd), F32),
+            pltpu.VMEM((n_en, 1, 3 * hd), F32),
+            pltpu.VMEM((n_fs, 1, 3 * hd), F32),
             pltpu.VMEM((n_text, n_slots), BF16),
             pltpu.VMEM((hd, seq), BF16),
             pltpu.VMEM((hd, seq), F32),

time: 100 us -> 99.7 us (level)
  no operation moved by 1% of the time
where the time goes in v4:
time: 99.7 us; the launch traced here: 99.6 us
  Pallas kernels  99 us (99%)
    pallas_call x1, Pallas kernels, on_device(): pl.pallas_call(functools.partial(kernel, sizes), out_shape=(pltpu.VMEM((3...  97.7 us

profile of v4, /device:TPU:6, one launch (start us, length us, event | category | flops | bytes accessed | tf_op | source)
XLA Modules:
  0.0 99.6 jit_solution(4884478059290742134)
XLA Ops:
  0.6 97.7 %shard_map.94 = (bf16[3,128,2048]{2,1,0:T(8,128)(2,1)S(1)}, bf16[16,2,2048]{2,1,0:T(2,128)(2,1)S(1)}, f32[3,128]{1,0:T(4,128)S(1)}) custom-call(bf16[3,128,2048]{2,1,0:T(8,128)(2,1)} %bitcast.11, bf16[128,2048]{1,0:T(8,128)(2,1)} %bitcast.12, bf16[16,2,2048]{2,1,0:T(2,128)(2,1)} %txt.1, s32[1,16]{1,0:T(1,128)} %bitcast.13, f32[1,128]{1,0:T(1,128)} %bitcast.14, ...), custom_call_target="tpu_custom_call" | custom-call | tf_op jit(solution)/shard_map/pallas_call | solution.py:559
  98.3 1.3 %shard_map.95 = (bf16[3,128,2048]{2,1,0:T(8,128)(2,1)}, bf16[16,2,2048]{2,1,0:T(2,128)(2,1)}, f32[3,128]{1,0:T(4,128)}) custom-call(bf16[3,128,2048]{2,1,0:T(8,128)(2,1)S(1)} %get-tuple-element.9.img, bf16[16,2,2048]{2,1,0:T(2,128)(2,1)S(1)} %get-tuple-element.10.txt, f32[3,128]{1,0:T(4,128)S(1)} %get-tuple-element.11.gain), custom_call_target="tpu_custom_call" | custom-call | tf_op jit(solution)/shard_map/pallas_call | solution.py:628

commit v5 on v4

--- a/solution.py
+++ b/solution.py
@@ -284,22 +284,24 @@
         def _():
             text_sends_to(step)
 
-    for step in range(1, n_sp - 1):
-
-        @pl.when(sp + step < n_sp - 1)
+    late = n_sp - 3
+
+    for step in range(1, late):
+
+        @pl.when(sp + step < late)
         def _():
             pl.semaphore_wait(above.at[step], 1)
             text_sends_to(step)
 
     for step in z_steps:
 
-        @pl.when(sp + step != n_sp - 1)
+        @pl.when(jnp.logical_or(sp + step < late, sp + step >= n_sp))
         def _():
             head_sends_to(step)
 
     for step in range(1, n_sp):
 
-        @pl.when(sp + step == n_sp - 1)
+        @pl.when(jnp.logical_and(sp + step >= late, sp + step < n_sp))
         def _():
             pl.semaphore_wait(above.at[step], 1)
             text_sends_to(step)

time: 99.7 us -> 99.6 us (level)
  no operation moved by 1% of the time
where the time goes in v5:
time: 99.6 us; the launch traced here: 99.5 us
  Pallas kernels  98.9 us (99%)
    pallas_call x1, Pallas kernels, on_device(): pl.pallas_call(functools.partial(kernel, sizes), out_shape=(pltpu.VMEM((3...  97.6 us

profile of v5, /device:TPU:6, one launch (start us, length us, event | category | flops | bytes accessed | tf_op | source)
XLA Modules:
  0.0 99.5 jit_solution(13670958649270061249)
XLA Ops:
  0.6 97.6 %shard_map.94 = (bf16[3,128,2048]{2,1,0:T(8,128)(2,1)S(1)}, bf16[16,2,2048]{2,1,0:T(2,128)(2,1)S(1)}, f32[3,128]{1,0:T(4,128)S(1)}) custom-call(bf16[3,128,2048]{2,1,0:T(8,128)(2,1)} %bitcast.11, bf16[128,2048]{1,0:T(8,128)(2,1)} %bitcast.12, bf16[16,2,2048]{2,1,0:T(2,128)(2,1)} %txt.1, s32[1,16]{1,0:T(1,128)} %bitcast.13, f32[1,128]{1,0:T(1,128)} %bitcast.14, ...), custom_call_target="tpu_custom_call" | custom-call | tf_op jit(solution)/shard_map/pallas_call | solution.py:561
  98.2 1.3 %shard_map.95 = (bf16[3,128,2048]{2,1,0:T(8,128)(2,1)}, bf16[16,2,2048]{2,1,0:T(2,128)(2,1)}, f32[3,128]{1,0:T(4,128)}) custom-call(bf16[3,128,2048]{2,1,0:T(8,128)(2,1)S(1)} %get-tuple-element.9.img, bf16[16,2,2048]{2,1,0:T(2,128)(2,1)S(1)} %get-tuple-element.10.txt, f32[3,128]{1,0:T(4,128)S(1)} %get-tuple-element.11.gain), custom_call_target="tpu_custom_call" | custom-call | tf_op jit(solution)/shard_map/pallas_call | solution.py:630
